TPU v7x, 256 devices: a whole 4x4x8 slice. The times are simulated.
256 devices in a mesh: sec: 16 (over x, y), grp: 16 (over z, core).
Axes of the slice: x: 4, y: 4, z: 8, core: 2. Of those that a mesh axis runs over, the one named last changes fastest.
Arguments:
- queries: bfloat16 [32768, 2048], P(('sec', 'grp')), may hold values from -6 to 6
- keys: bfloat16 [32768, 2048], P(('sec', 'grp')), may hold values from -6 to 6
- values: bfloat16 [32768, 2048], P(('sec', 'grp')), may hold values from -6 to 6
- dout: bfloat16 [32768, 2048], P(('sec', 'grp')), may hold values from -48 to 48
- history: bfloat16 [1024, 2, 2048], P('sec', None, 'grp'), may hold values from -6 to 6
- context: int32 [16], replicated, may hold values from 1 to 1024, as said below
Outputs:
- grad_queries: bfloat16 [32768, 2048], P(('sec', 'grp'))
- grad_keys: bfloat16 [32768, 2048], P(('sec', 'grp'))
- grad_values: bfloat16 [32768, 2048], P(('sec', 'grp'))
- grad_history: float32 [1024, 2, 2048], P('sec', None, 'grp')
Inputs may be any that keep to these rules, and one draw needn't show every extreme that they name: Section s attends to history rows 0 to context[s] - 1; some section attends to all 1024 rows.
All inputs are finite; a program needn't handle non-finite values.
Results may differ from a plain program's by a relative error of at most 0.017.
Values may be sent and summed in bfloat16 or wider, within the bound.
A program may use at most 64 MiB of HBM per device.

v0:
```python
import jax
import jax.numpy as jnp
from jax import lax
from jax.sharding import PartitionSpec as P

HD = 128


def swap_heads(queries, keys, values, dout):
    return (
        lax.all_to_all(queries, "grp", split_axis=1, concat_axis=0, tiled=True),
        lax.all_to_all(keys, "grp", split_axis=1, concat_axis=0, tiled=True),
        lax.all_to_all(values, "grp", split_axis=1, concat_axis=0, tiled=True),
        lax.all_to_all(dout, "grp", split_axis=1, concat_axis=0, tiled=True),
    )


def fetch_history(history):
    return lax.all_gather(history, "sec", axis=0, tiled=True)


def on_device(queries, keys, values, dout, history, context):
    q_loc, k_loc, v_loc, g_loc = swap_heads(queries, keys, values, dout)
    whole_hist = fetch_history(history)
    seq_rows = q_loc.shape[0]
    head_dev = q_loc.shape[1] // HD
    hist_rows = whole_hist.shape[0]
    scale = HD ** (-0.5)
    ctx = lax.dynamic_index_in_dim(context, lax.axis_index("sec"), 0, keepdims=False)
    q_heads = q_loc.reshape(seq_rows, head_dev, HD)
    g_heads = g_loc.reshape(seq_rows, head_dev, HD)
    key_list = jnp.concatenate(
        [k_loc.reshape(seq_rows, head_dev, HD), whole_hist[:, 0].reshape(hist_rows, head_dev, HD)],
        0,
    )
    val_list = jnp.concatenate(
        [v_loc.reshape(seq_rows, head_dev, HD), whole_hist[:, 1].reshape(hist_rows, head_dev, HD)],
        0,
    )
    visible = jnp.arange(seq_rows + hist_rows, dtype=jnp.int32) < seq_rows + ctx
    block = min(512, seq_rows)
    blocks = seq_rows // block

    def step(carry, index):
        key_acc, val_acc = carry
        start = index * block
        q_block = lax.dynamic_slice_in_dim(q_heads, start, block, 0)
        g_block = lax.dynamic_slice_in_dim(g_heads, start, block, 0)
        scores = (
            jnp.einsum("bhd,khd->hbk", q_block, key_list, preferred_element_type=jnp.float32)
            * scale
        )
        scores = jnp.where(visible[None, None, :], scores, -jnp.inf)
        top = jnp.max(scores, axis=-1, keepdims=True)
        lse = top + jnp.log(jnp.sum(jnp.exp(scores - top), axis=-1, keepdims=True))
        probs = jnp.exp(scores - lse)
        probs_low = probs.astype(jnp.bfloat16)
        out = jnp.einsum("hbk,khd->hbd", probs_low, val_list, preferred_element_type=jnp.float32)
        delta = jnp.sum(
            jnp.transpose(g_block, (1, 0, 2)).astype(jnp.float32) * out, axis=-1, keepdims=True
        )
        dprobs = jnp.einsum("bhd,khd->hbk", g_block, val_list, preferred_element_type=jnp.float32)
        dscores = (probs * (dprobs - delta) * scale).astype(jnp.bfloat16)
        grad_block = jnp.einsum(
            "hbk,khd->bhd", dscores, key_list, preferred_element_type=jnp.float32
        )
        key_acc = key_acc + jnp.einsum(
            "hbk,bhd->khd", dscores, q_block, preferred_element_type=jnp.float32
        )
        val_acc = val_acc + jnp.einsum(
            "hbk,bhd->khd", probs_low, g_block, preferred_element_type=jnp.float32
        )
        return ((key_acc, val_acc), grad_block.astype(jnp.bfloat16))

    empty = jnp.zeros((seq_rows + hist_rows, head_dev, HD), jnp.float32)
    (key_acc, val_acc), grad_blocks = lax.scan(
        step, (empty, empty), jnp.arange(blocks, dtype=jnp.int32)
    )
    grad_q = grad_blocks.reshape(seq_rows, head_dev * HD)
    grad_k = key_acc[:seq_rows].reshape(seq_rows, head_dev * HD).astype(jnp.bfloat16)
    grad_v = val_acc[:seq_rows].reshape(seq_rows, head_dev * HD).astype(jnp.bfloat16)
    back_q, back_k, back_v = (
        lax.all_to_all(grad_q, "grp", split_axis=0, concat_axis=1, tiled=True),
        lax.all_to_all(grad_k, "grp", split_axis=0, concat_axis=1, tiled=True),
        lax.all_to_all(grad_v, "grp", split_axis=0, concat_axis=1, tiled=True),
    )
    hist_terms = jnp.stack(
        [
            key_acc[seq_rows:].reshape(hist_rows, head_dev * HD),
            val_acc[seq_rows:].reshape(hist_rows, head_dev * HD),
        ],
        axis=1,
    )
    own_rows = history.shape[0]
    total = lax.psum(hist_terms.astype(jnp.bfloat16), "sec").astype(jnp.float32)
    grad_history = lax.dynamic_slice_in_dim(total, lax.axis_index("sec") * own_rows, own_rows, 0)
    return (back_q, back_k, back_v, grad_history)


def solution(mesh):
    return jax.shard_map(
        on_device,
        mesh=mesh,
        in_specs=(
            P(("sec", "grp"), None),
            P(("sec", "grp"), None),
            P(("sec", "grp"), None),
            P(("sec", "grp"), None),
            P("sec", None, "grp"),
            P(),
        ),
        out_specs=(
            P(("sec", "grp"), None),
            P(("sec", "grp"), None),
            P(("sec", "grp"), None),
            P("sec", None, "grp"),
        ),
        check_vma=False,
    )
```

profile of v0, /device:TPU:1, one launch (start us, length us, event | category | flops | bytes accessed | tf_op | source)
XLA Modules:
  0.0 363.0 jit_solution(3785622865981260730)
XLA Ops:
  7.2 2.1 copy.63
  9.3 10.0 %all-to-all-start.3 = ((bf16[128,16,128]{0,2,1:T(8,128)(2,1)}), bf16[128,16,128]{0,2,1:T(8,128)(2,1)S(1)}, u32[]{:S(2)}, u32[]{:S(2)}) async-start(bf16[128,16,128]{0,2,1:T(8,128)(2,1)} %bitcast.9), calls=%async_computation.3 | async-start | bytes 1048576 | tf_op jit(solution)/shard_map/all_to_all | solution.py:13
  19.3 2.1 copy.58
  21.4 15.2 %all-to-all-done.3 = bf16[128,16,128]{0,2,1:T(8,128)(2,1)S(1)} async-done(((bf16[128,16,128]{0,2,1:T(8,128)(2,1)}), bf16[128,16,128]{0,2,1:T(8,128)(2,1)S(1)}, u32[]{:S(2)}, u32[]{:S(2)}) %all-to-all-start.3) | async-done | bytes 524320 | tf_op jit(solution)/shard_map/all_to_all | solution.py:13
  36.6 3.5 all-to-all-start.1
  41.1 15.7 %all-to-all-done.1 = bf16[128,16,128]{0,2,1:T(8,128)(2,1)S(1)} async-done(((bf16[128,16,128]{0,2,1:T(8,128)(2,1)}), bf16[128,16,128]{0,2,1:T(8,128)(2,1)S(1)}, u32[]{:S(2)}, u32[]{:S(2)}) %all-to-all-start.1) | async-done | bytes 524320 | tf_op jit(solution)/shard_map/all_to_all | solution.py:12
  56.8 3.5 all-to-all-start
  61.3 15.7 %all-to-all-done = bf16[128,16,128]{0,2,1:T(8,128)(2,1)S(1)} async-done(((bf16[128,16,128]{0,2,1:T(8,128)(2,1)}), bf16[128,16,128]{0,2,1:T(8,128)(2,1)S(1)}, u32[]{:S(2)}, u32[]{:S(2)}) %all-to-all-start) | async-done | bytes 524320 | tf_op jit(solution)/shard_map/all_to_all | solution.py:11
  77.0 4.1 %all-to-all-start.2 = ((bf16[128,16,128]{0,2,1:T(8,128)(2,1)}), bf16[128,16,128]{0,2,1:T(8,128)(2,1)}, u32[]{:S(2)}, u32[]{:S(2)}) async-start(bf16[128,16,128]{0,2,1:T(8,128)(2,1)} %bitcast.6), calls=%async_computation.2 | async-start | bytes 1048576 | tf_op jit(solution)/shard_map/all_to_all | solution.py:14
  82.5 20.8 %all_gather.3 = bf16[1024,2,128]{2,0,1:T(8,128)(2,1)S(1)} all-gather(bf16[64,2,128]{2,0,1:T(8,128)(2,1)S(1)} %copy.60), channel_id=1, replica_groups=mesh['sec'=16,'grp'=16] {'sec'}, dimensions={0}, use_global_device_ids=true | all-gather | bytes 557056 | tf_op jit(solution)/shard_map/all_gather | solution.py:19
  108.5 2.0 copy.62
  110.5 89.7 %while.15 = (s32[]{:T(128)}, f32[3072,1,128]{0,2,1:T(8,128)S(1)}, f32[3072,1,128]{0,2,1:T(8,128)}, bf16[4,512,1,128]{3,1,2,0:T(8,128)(2,1)}, s32[4]{0:T(128)S(1)...) while((s32[]{:T(128)}, f32[3072,1,128]{0,2,1:T(8,128)S(1)}, ...), condition=%wide.region_4.5_spmd.clone, body=%wide.region_0.4_spmd.clone.sunk | while | flops 2439776256 | bytes 102003480 | solution.py:76
  111.8 2.0 fusion.51
  117.4 5.2 %fusion.54 = f32[3072,1,128]{0,2,1:T(8,128)} fusion(f32[3072,1,128]{0,2,1:T(8,128)} %get-tuple-element.230, pred[]{:T(512)S(6)} %compare.3, bf16[512,1,128]{2,0,1:T(8,128)(2,1)S(1)} %constant_dynamic-slice_fusion.2, f32[512,3072]{1,0:T(8,128)} %copy-done, f32[512]{0:T(512)S(1)} %log_add_fusion.2), kind=kOutput, calls=%fused_computation.9.clone.1 | convolution fusion | flops 406585344 | bytes 9570305 | tf_op jit(solution)/shard_map/while/body/eval_jaxpr/hbk,bhd->khd/dot_general | solution.py:70
  122.8 4.2 %fusion.52 = f32[512]{0:T(512)S(1)} fusion(bf16[3072,1,128]{2,0,1:T(8,128)(2,1)S(1)} %get-tuple-element.250, bf16[512,1,128]{0,2,1:T(8,128)(2,1)S(1)} %copy.77, f32[512,3072]{1,0:T(8,128)} %copy-done, f32[512]{0:T(512)S(1)} %log_add_fusion.2), kind=kOutput, calls=%fused_computation.12.clone.1 | convolution fusion | flops 405995008 | bytes 7213056 | tf_op jit(solution)/shard_map/while/body/eval_jaxpr/hbk,khd->hbd/dot_general | solution.py:58
  127.4 1.9 multiply_convert_fusion.2
  133.9 2.0 fusion.51
  139.5 5.7 %fusion.54 = f32[3072,1,128]{0,2,1:T(8,128)} fusion(f32[3072,1,128]{0,2,1:T(8,128)} %get-tuple-element.230, pred[]{:T(512)S(6)} %compare.3, bf16[512,1,128]{2,0,1:T(8,128)(2,1)S(1)} %constant_dynamic-slice_fusion.2, f32[512,3072]{1,0:T(8,128)} %copy-done, f32[512]{0:T(512)S(1)} %log_add_fusion.2), kind=kOutput, calls=%fused_computation.9.clone.1 | convolution fusion | flops 406585344 | bytes 9570305 | tf_op jit(solution)/shard_map/while/body/eval_jaxpr/hbk,bhd->khd/dot_general | solution.py:70
  145.3 4.2 %fusion.52 = f32[512]{0:T(512)S(1)} fusion(bf16[3072,1,128]{2,0,1:T(8,128)(2,1)S(1)} %get-tuple-element.250, bf16[512,1,128]{0,2,1:T(8,128)(2,1)S(1)} %copy.77, f32[512,3072]{1,0:T(8,128)} %copy-done, f32[512]{0:T(512)S(1)} %log_add_fusion.2), kind=kOutput, calls=%fused_computation.12.clone.1 | convolution fusion | flops 405995008 | bytes 7213056 | tf_op jit(solution)/shard_map/while/body/eval_jaxpr/hbk,khd->hbd/dot_general | solution.py:58
  156.4 2.0 fusion.51
  162.1 5.7 %fusion.54 = f32[3072,1,128]{0,2,1:T(8,128)} fusion(f32[3072,1,128]{0,2,1:T(8,128)} %get-tuple-element.230, pred[]{:T(512)S(6)} %compare.3, bf16[512,1,128]{2,0,1:T(8,128)(2,1)S(1)} %constant_dynamic-slice_fusion.2, f32[512,3072]{1,0:T(8,128)} %copy-done, f32[512]{0:T(512)S(1)} %log_add_fusion.2), kind=kOutput, calls=%fused_computation.9.clone.1 | convolution fusion | flops 406585344 | bytes 9570305 | tf_op jit(solution)/shard_map/while/body/eval_jaxpr/hbk,bhd->khd/dot_general | solution.py:70
  167.9 4.2 %fusion.52 = f32[512]{0:T(512)S(1)} fusion(bf16[3072,1,128]{2,0,1:T(8,128)(2,1)S(1)} %get-tuple-element.250, bf16[512,1,128]{0,2,1:T(8,128)(2,1)S(1)} %copy.77, f32[512,3072]{1,0:T(8,128)} %copy-done, f32[512]{0:T(512)S(1)} %log_add_fusion.2), kind=kOutput, calls=%fused_computation.12.clone.1 | convolution fusion | flops 405995008 | bytes 7213056 | tf_op jit(solution)/shard_map/while/body/eval_jaxpr/hbk,khd->hbd/dot_general | solution.py:58
  179.0 2.0 fusion.51
  184.6 5.7 %fusion.54 = f32[3072,1,128]{0,2,1:T(8,128)} fusion(f32[3072,1,128]{0,2,1:T(8,128)} %get-tuple-element.230, pred[]{:T(512)S(6)} %compare.3, bf16[512,1,128]{2,0,1:T(8,128)(2,1)S(1)} %constant_dynamic-slice_fusion.2, f32[512,3072]{1,0:T(8,128)} %copy-done, f32[512]{0:T(512)S(1)} %log_add_fusion.2), kind=kOutput, calls=%fused_computation.9.clone.1 | convolution fusion | flops 406585344 | bytes 9570305 | tf_op jit(solution)/shard_map/while/body/eval_jaxpr/hbk,bhd->khd/dot_general | solution.py:70
  190.4 4.2 %fusion.52 = f32[512]{0:T(512)S(1)} fusion(bf16[3072,1,128]{2,0,1:T(8,128)(2,1)S(1)} %get-tuple-element.250, bf16[512,1,128]{0,2,1:T(8,128)(2,1)S(1)} %copy.77, f32[512,3072]{1,0:T(8,128)} %copy-done, f32[512]{0:T(512)S(1)} %log_add_fusion.2), kind=kOutput, calls=%fused_computation.12.clone.1 | convolution fusion | flops 405995008 | bytes 7213056 | tf_op jit(solution)/shard_map/while/body/eval_jaxpr/hbk,khd->hbd/dot_general | solution.py:58
  195.0 1.9 multiply_convert_fusion.2
  201.4 1.9 slice.30
  203.3 9.8 %all-to-all-start.5 = ((bf16[16,128,128]{2,1,0:T(8,128)(2,1)}), bf16[16,128,128]{2,1,0:T(8,128)(2,1)S(1)}, u32[]{:S(2)}, u32[]{:S(2)}) async-start(bf16[16,128,128]{2,1,0:T(8,128)(2,1)} %bitcast.16), calls=%async_computation.5 | async-start | bytes 1048576 | tf_op jit(solution)/shard_map/all_to_all | solution.py:84
  213.5 16.9 %all-to-all-done.5 = bf16[16,128,128]{2,1,0:T(8,128)(2,1)S(1)} async-done(((bf16[16,128,128]{2,1,0:T(8,128)(2,1)}), bf16[16,128,128]{2,1,0:T(8,128)(2,1)S(1)}, u32[]{:S(2)}, u32[]{:S(2)}) %all-to-all-start.5) | async-done | bytes 524320 | tf_op jit(solution)/shard_map/all_to_all | solution.py:84
  230.4 20.0 %all_to_all.115 = bf16[16,128,128]{2,1,0:T(8,128)(2,1)S(1)} all-to-all(bf16[16,128,128]{2,1,0:T(8,128)(2,1)S(1)} %bitcast.113), channel_id=1, replica_groups=mesh['sec'=16,'grp'=16] {'grp'}, dimensions={0} | all-to-all | bytes 1048576 | tf_op jit(solution)/shard_map/all_to_all | solution.py:85
  250.4 3.5 all-to-all-start.4
  254.9 95.9 %all-reduce.2.cloned.1.call-done = bf16[1024,2,128]{2,0,1:T(8,128)(2,1)} async-done(((bf16[1024,2,128]{2,0,1:T(8,128)(2,1)}), bf16[1024,2,128]{2,0,1:T(8,128)(2,1)}) %all-reduce.2.cloned.1.call-update) | async-done | bytes 524304 | tf_op jit(solution)/shard_map/psum | solution.py:95
  (92 shorter events, 51.7 us)
Async XLA Ops:
  7.2 32.9 %copy-start.3 = (bf16[128,2048]{1,0:T(8,128)(2,1)S(1)}, bf16[128,2048]{1,0:T(8,128)(2,1)}, u32[]{:S(2)}) copy-start(bf16[128,2048]{1,0:T(8,128)(2,1)} %param.8) | copy-start | bytes 1572868
  7.2 53.1 %copy-start.4 = (bf16[128,2048]{1,0:T(8,128)(2,1)S(1)}, bf16[128,2048]{1,0:T(8,128)(2,1)}, u32[]{:S(2)}) copy-start(bf16[128,2048]{1,0:T(8,128)(2,1)} %param.11) | copy-start | bytes 1572868
  9.3 27.3 %all-to-all-start.3 = ((bf16[128,16,128]{0,2,1:T(8,128)(2,1)}), bf16[128,16,128]{0,2,1:T(8,128)(2,1)S(1)}, u32[]{:S(2)}, u32[]{:S(2)}) async-start(bf16[128,16,128]{0,2,1:T(8,128)(2,1)} %bitcast.9), calls=%async_computation.3 | async-start | bytes 1048576 | tf_op jit(solution)/shard_map/all_to_all | solution.py:13
  19.3 61.9 %copy-start.5 = (bf16[64,2,128]{2,1,0:T(2,128)(2,1)S(1)}, bf16[64,2,128]{2,1,0:T(2,128)(2,1)}, u32[]{:S(2)}) copy-start(bf16[64,2,128]{2,1,0:T(2,128)(2,1)} %param.12) | copy-start | bytes 98308
  19.3 61.9 %copy-start.6 = (s32[16]{0:T(128)S(1)}, s32[16]{0:T(128)}, u32[]{:S(2)}) copy-start(s32[16]{0:T(128)} %param.13) | copy-start | bytes 196
  36.6 20.2 %all-to-all-start.1 = ((bf16[128,16,128]{0,2,1:T(8,128)(2,1)}), bf16[128,16,128]{0,2,1:T(8,128)(2,1)S(1)}, u32[]{:S(2)}, u32[]{:S(2)}) async-start(bf16[128,16,128]{0,2,1:T(8,128)(2,1)} %bitcast.3), calls=%async_computation.1 | async-start | bytes 1048576 | tf_op jit(solution)/shard_map/all_to_all | solution.py:12
  56.8 20.2 %all-to-all-start = ((bf16[128,16,128]{0,2,1:T(8,128)(2,1)}), bf16[128,16,128]{0,2,1:T(8,128)(2,1)S(1)}, u32[]{:S(2)}, u32[]{:S(2)}) async-start(bf16[128,16,128]{0,2,1:T(8,128)(2,1)} %bitcast), calls=%async_computation | async-start | bytes 1048576 | tf_op jit(solution)/shard_map/all_to_all | solution.py:11
  77.0 31.4 %all-to-all-start.2 = ((bf16[128,16,128]{0,2,1:T(8,128)(2,1)}), bf16[128,16,128]{0,2,1:T(8,128)(2,1)}, u32[]{:S(2)}, u32[]{:S(2)}) async-start(bf16[128,16,128]{0,2,1:T(8,128)(2,1)} %bitcast.6), calls=%async_computation.2 | async-start | bytes 1048576 | tf_op jit(solution)/shard_map/all_to_all | solution.py:14
  113.8 2.7 copy-start
  122.8 4.6 %copy-start.1 = (f32[512,3072]{1,0:T(8,128)S(1)}, f32[512,3072]{1,0:T(8,128)}, u32[]{:S(2)}) copy-start(f32[512,3072]{1,0:T(8,128)} %copy-done) | copy-start | bytes 18874372 | tf_op jit(solution)/shard_map/while
  135.9 2.7 copy-start
  145.3 4.6 %copy-start.1 = (f32[512,3072]{1,0:T(8,128)S(1)}, f32[512,3072]{1,0:T(8,128)}, u32[]{:S(2)}) copy-start(f32[512,3072]{1,0:T(8,128)} %copy-done) | copy-start | bytes 18874372 | tf_op jit(solution)/shard_map/while
  158.5 2.7 copy-start
  167.8 4.6 %copy-start.1 = (f32[512,3072]{1,0:T(8,128)S(1)}, f32[512,3072]{1,0:T(8,128)}, u32[]{:S(2)}) copy-start(f32[512,3072]{1,0:T(8,128)} %copy-done) | copy-start | bytes 18874372 | tf_op jit(solution)/shard_map/while
  181.0 2.7 copy-start
  190.4 4.6 %copy-start.1 = (f32[512,3072]{1,0:T(8,128)S(1)}, f32[512,3072]{1,0:T(8,128)}, u32[]{:S(2)}) copy-start(f32[512,3072]{1,0:T(8,128)} %copy-done) | copy-start | bytes 18874372 | tf_op jit(solution)/shard_map/while
  200.2 12.9 %copy-start.2 = (f32[3072,1,128]{0,2,1:T(8,128)S(1)}, f32[3072,1,128]{0,2,1:T(8,128)}, u32[]{:S(2)}) copy-start(f32[3072,1,128]{0,2,1:T(8,128)} %get-tuple-element.60) | copy-start | bytes 4718596
  203.3 27.1 %all-to-all-start.5 = ((bf16[16,128,128]{2,1,0:T(8,128)(2,1)}), bf16[16,128,128]{2,1,0:T(8,128)(2,1)S(1)}, u32[]{:S(2)}, u32[]{:S(2)}) async-start(bf16[16,128,128]{2,1,0:T(8,128)(2,1)} %bitcast.16), calls=%async_computation.5 | async-start | bytes 1048576 | tf_op jit(solution)/shard_map/all_to_all | solution.py:84
  213.1 40.9 %slice-start = ((bf16[3072,1,128]{2,0,1:T(8,128)(2,1)}), bf16[1024,1,128]{2,0,1:T(8,128)(2,1)S(1)}, s32[]{:S(2)}) async-start(bf16[3072,1,128]{2,0,1:T(8,128)(2,1)} %copy.67), calls=%async_computation.8 | async-start | bytes 524288 | tf_op jit(solution)/shard_map/slice | solution.py:89
  250.4 104.4 %all-to-all-start.4 = ((bf16[16,128,128]{2,1,0:T(8,128)(2,1)}), bf16[16,128,128]{2,1,0:T(8,128)(2,1)S(1)}, u32[]{:S(2)}, u32[]{:S(2)}) async-start(bf16[16,128,128]{2,1,0:T(8,128)(2,1)} %bitcast.13), calls=%async_computation.4 | async-start | bytes 1048576 | tf_op jit(solution)/shard_map/all_to_all | solution.py:83
  253.9 96.9 %all-reduce.2.cloned.1.call-start = ((), (), s32[]{:S(2)}) async-start(), calls=%async_computation.7 | async-start | bytes 1048576 | tf_op jit(solution)/shard_map/psum | solution.py:95
Sparse Core Ops, SparseCore 0:
  258.5 92.2 all-reduce.1
where the time goes:
time: 364 us; the launch traced here: 363 us
  waiting for transfers between devices  159 us (44%)
  matrix products  68.1 us (19%)
  blocking collectives  40.8 us (11%)
  local copies, waits for them, and re-layouts  35.5 us (10%)
  starting transfers between devices  34.4 us (9%)
  between operations  14.9 us (4%)
  other arithmetic  7.01 us (2%)
    psum x1, waiting for transfers between devices, on_device(): total = lax.psum(hist_terms.astype(jnp.bfloat16), 'sec').astype(jnp.float32)  95.9 us
    dot_general x4, matrix products, step(): jnp.einsum('hbk,bhd->khd', probs_low, g_block, preferred_element_type=jnp...  22.2 us
    all_gather x1, blocking collectives, fetch_history(): return lax.all_gather(history, 'sec', axis=0, tiled=True)  20.8 us
    all_to_all x1, blocking collectives, on_device(): lax.all_to_all(grad_v, 'grp', split_axis=0, concat_axis=1, tiled=True)  20 us
    all_to_all x1, waiting for transfers between devices, on_device(): lax.all_to_all(grad_k, 'grp', split_axis=0, concat_axis=1, tiled=True)  16.9 us
    dot_general x4, matrix products, step(): jnp.einsum('hbk,khd->hbd', probs_low, val_list, preferred_element_type=jn...  16.8 us
    all_to_all x1, waiting for transfers between devices, swap_heads(): lax.all_to_all(queries, 'grp', split_axis=1, concat_axis=0, tiled=True)  15.7 us
    all_to_all x1, waiting for transfers between devices, swap_heads(): lax.all_to_all(keys, 'grp', split_axis=1, concat_axis=0, tiled=True)  15.7 us
  transfers between devices with their start and end apart: 7, of which 5 were waited for; matrix products, arithmetic and copies ran while one was open for 4% of the time, Pallas kernels for 0%

commit v1 on v0

v1 whole, which is shorter than its diff:
```python
import functools
import math

import jax
import jax.numpy as jnp
from jax import lax
from jax.experimental import pallas as pl
from jax.experimental.pallas import tpu as pltpu
from jax.sharding import PartitionSpec as P

HD = 128
MESH = pl.DeviceIdType.MESH
NT = (((1,), (1,)), ((), ()))
NN = (((1,), (0,)), ((), ()))
F32 = jnp.float32
BF = jnp.bfloat16
SCALE = HD ** (-0.5)
LOG2E = math.log2(math.e)
KC = 512


def dot(a, b, dims=NN):
    return lax.dot_general(a, b, dims, preferred_element_type=F32)


def kernel(
    secs,
    grps,
    q_in,
    k_in,
    v_in,
    g_in,
    h_in,
    ctx_in,
    gq_out,
    gk_out,
    gv_out,
    gh_out,
    qb,
    gb,
    kb,
    vb,
    kt,
    sb,
    eb,
    db,
    dka,
    dva,
    dqs,
    dks,
    dvs,
    hbk,
    hbv,
    in_send,
    in_recv,
    h_send,
    h_recv,
    out_send,
    out_recv,
    gh_send,
    gh_recv,
):
    own = q_in.shape[0]
    chips = grps // 2
    block = 2 * own
    seq = grps * own
    hown = h_in.shape[0]
    keys = seq + secs * hown
    parts = keys // KC
    sec = lax.axis_index("sec")
    grp = lax.axis_index("grp")
    z, core = grp // 2, grp % 2

    def shift(t):
        return ((t + 1) // 2) * (2 * (t % 2) - 1) + chips

    def to_chip(t):
        return (z + shift(t)) % chips

    def from_chip(t):
        return (z - shift(t) + 2 * chips) % chips

    def device(chip, dc):
        return 2 * chip + (core + dc) % 2

    def cols(d):
        return pl.ds(pl.multiple_of(d * HD, HD), HD)

    def rows(d, n, base=0):
        return pl.ds(pl.multiple_of(base + d * n, n), n)

    barrier = pltpu.get_barrier_semaphore()

    @pl.loop(1, grps)
    def _(i):
        pl.semaphore_signal(
            barrier, 1, device_id=(sec, (grp + i) % grps), device_id_type=MESH
        )

    @pl.loop(1, secs)
    def _(i):
        pl.semaphore_signal(
            barrier, 1, device_id=((sec + i) % secs, grp), device_id_type=MESH
        )

    pl.semaphore_wait(barrier, grps + secs - 2)

    def in_copy(a, src, dst, t, dc):
        to = device(to_chip(t), dc)
        return pltpu.make_async_remote_copy(
            src.at[:, cols(to)],
            dst.at[rows(grp, own)],
            in_send.at[a, 2 * t + dc],
            in_recv.at[a, 2 * t + dc],
            device_id=(sec, to),
            device_id_type=MESH,
        )

    def in_local(a, src, dst):
        return pltpu.make_async_copy(
            src.at[:, cols(grp)], dst.at[rows(grp, own)], in_recv.at[a, 0]
        )

    arrays = ((0, k_in, kb), (1, v_in, vb), (2, q_in, qb), (3, g_in, gb))

    def h_copy(a, dst, i):
        return pltpu.make_async_remote_copy(
            h_in.at[:, pl.ds(a * HD, HD)],
            dst.at[rows(sec, hown, seq)],
            h_send.at[a, i],
            h_recv.at[a, i],
            device_id=((sec + i) % secs, grp),
            device_id_type=MESH,
        )

    def h_local(a, dst):
        return pltpu.make_async_copy(
            h_in.at[:, pl.ds(a * HD, HD)], dst.at[rows(sec, hown, seq)], h_recv.at[a, 0]
        )

    def start_in(first, last):
        for a, src, dst in arrays[first:last]:
            in_local(a, src, dst).start()
        for a, src, dst in arrays[first:last]:
            in_copy(a, src, dst, 0, 1).start()

        @pl.loop(1, chips)
        def _(t):
            for a, src, dst in arrays[first:last]:
                in_copy(a, src, dst, t, 0).start()
                in_copy(a, src, dst, t, 1).start()

    start_in(0, 2)
    for a, dst in ((0, kb), (1, vb)):
        h_local(a, dst).start()

    @pl.loop(1, secs)
    def _(i):
        h_copy(0, kb, i).start()
        h_copy(1, vb, i).start()

    start_in(2, 4)

    dka[...] = jnp.zeros_like(dka)
    dva[...] = jnp.zeros_like(dva)
    ctx = ctx_in[sec]

    def wait_in(a, src, dst, t, dc):
        if dc == 0:

            @pl.when(t == 0)
            def _():
                in_local(a, src, dst).wait()

            @pl.when(t > 0)
            def _():
                in_copy(a, src, dst, t, dc).wait_recv()
        else:
            in_copy(a, src, dst, t, dc).wait_recv()

    @pl.loop(0, chips)
    def _(t):
        for a, src, dst in arrays[:2]:
            for dc in range(2):
                wait_in(a, src, dst, t, dc)

    for a, dst in ((0, kb), (1, vb)):
        h_local(a, dst).wait()

    @pl.loop(1, secs)
    def _(i):
        h_copy(0, kb, i).wait_recv()
        h_copy(1, vb, i).wait_recv()

    for j in range(parts):
        kt[:, j * KC : (j + 1) * KC] = kb[j * KC : (j + 1) * KC, :].T

    def out_copy(a, src, dst, t, dc):
        to = device(from_chip(t), dc)
        return pltpu.make_async_remote_copy(
            src.at[rows(to, own)],
            dst.at[:, cols(grp)],
            out_send.at[a, 2 * t + dc],
            out_recv.at[a, 2 * t + dc],
            device_id=(sec, to),
            device_id_type=MESH,
        )

    def out_local(a, src, dst):
        return pltpu.make_async_copy(
            src.at[rows(grp, own)], dst.at[:, cols(grp)], out_recv.at[a, 0]
        )

    def start_out(a, src, dst, t):
        out_copy(a, src, dst, t, 1).start()

        @pl.when(t == 0)
        def _():
            out_local(a, src, dst).start()

        @pl.when(t > 0)
        def _():
            out_copy(a, src, dst, t, 0).start()

    @pl.loop(0, chips)
    def _(t):
        for a, src, dst in arrays[2:]:
            for dc in range(2):
                wait_in(a, src, dst, t, dc)
        here = rows(from_chip(t), block)
        q = qb[here, :]
        g = gb[here, :]
        top = jnp.full((8, block), -jnp.inf, F32)
        for j in range(parts):
            part = slice(j * KC, (j + 1) * KC)
            s = dot(kb[part, :], q, NT)
            if (j + 1) * KC > seq:
                row = lax.broadcasted_iota(jnp.int32, (KC, block), 0) + (j * KC - seq)
                s = jnp.where(row < ctx, s, -jnp.inf)
            sb[part, :] = s
            top = jnp.maximum(top, jnp.max(s.reshape(KC // 8, 8, block), axis=0))
        top = jnp.max(top, axis=0, keepdims=True)
        total = jnp.zeros((8, block), F32)
        delta = jnp.zeros((8, block), F32)
        for j in range(parts):
            part = slice(j * KC, (j + 1) * KC)
            e = jnp.exp2((sb[part, :] - top) * (SCALE * LOG2E))
            dp = dot(vb[part, :], g, NT)
            total = total + jnp.sum(e.reshape(KC // 8, 8, block), axis=0)
            delta = delta + jnp.sum((e * dp).reshape(KC // 8, 8, block), axis=0)
            eb[part, :] = e
            db[part, :] = dp
        inv = 1.0 / jnp.sum(total, axis=0, keepdims=True)
        delta = jnp.sum(delta, axis=0, keepdims=True) * inv
        inv_col = jnp.transpose(jnp.broadcast_to(inv, (HD, block)))
        gs = (g.astype(F32) * inv_col).astype(BF)
        qs = (q.astype(F32) * (inv_col * SCALE)).astype(BF)
        dqt = jnp.zeros((HD, block), F32)
        for j in range(parts):
            part = slice(j * KC, (j + 1) * KC)
            e = eb[part, :]
            ds = (e * (db[part, :] - delta)).astype(BF)
            dva[part, :] += dot(e.astype(BF), gs)
            dka[part, :] += dot(ds, qs)
            dqt = dqt + dot(kt[:, part], ds)
        dqs[here, :] = jnp.transpose(dqt * (inv * SCALE)).astype(BF)
        start_out(0, dqs, gq_out, t)

    def gh_copy(a, src, dst, i):
        to = (sec + i) % secs
        return pltpu.make_async_remote_copy(
            src.at[rows(to, hown, seq)],
            dst.at[rows(i, hown)],
            gh_send.at[a, i],
            gh_recv.at[a, i],
            device_id=(to, grp),
            device_id_type=MESH,
        )

    def gh_local(a, src, dst):
        return pltpu.make_async_copy(
            src.at[rows(sec, hown, seq)], dst.at[rows(0, hown)], gh_recv.at[a, 0]
        )

    hist_parts = ((0, dks, hbk), (1, dvs, hbv))
    dks[seq:, :] = dka[seq:, :].astype(BF)
    dvs[seq:, :] = dva[seq:, :].astype(BF)
    for a, src, dst in hist_parts:
        gh_local(a, src, dst).start()

    @pl.loop(1, secs)
    def _(i):
        for a, src, dst in hist_parts:
            gh_copy(a, src, dst, i).start()

    back = ((1, dks, gk_out), (2, dvs, gv_out))

    @pl.loop(0, chips)
    def _(t):
        here = rows(from_chip(t), block)
        dks[here, :] = dka[here, :].astype(BF)
        dvs[here, :] = dva[here, :].astype(BF)
        for a, src, dst in back:
            start_out(a, src, dst, t)

    for a, src, dst in hist_parts:
        gh_local(a, src, dst).wait()

    @pl.loop(1, secs)
    def _(i):
        for a, src, dst in hist_parts:
            gh_copy(a, src, dst, i).wait()

    for a, buf in ((0, hbk), (1, hbv)):
        acc = buf[0:hown, :].astype(F32)
        for i in range(1, secs):
            acc = acc + buf[i * hown : (i + 1) * hown, :].astype(F32)
        gh_out[:, a * HD : (a + 1) * HD] = acc

    @pl.loop(1, secs)
    def _(i):
        h_copy(0, kb, i).wait_send()
        h_copy(1, vb, i).wait_send()

    for a, src, dst in arrays:
        in_copy(a, src, dst, 0, 1).wait_send()
    for a, src, dst in ((0, dqs, gq_out),) + back:
        out_copy(a, src, dst, 0, 1).wait()
        out_local(a, src, dst).wait()

    @pl.loop(1, chips)
    def _(t):
        for dc in range(2):
            for a, src, dst in arrays:
                in_copy(a, src, dst, t, dc).wait_send()
            for a, src, dst in ((0, dqs, gq_out),) + back:
                out_copy(a, src, dst, t, dc).wait()


def on_device(secs, grps, queries, keys, values, dout, history, context):
    own = queries.shape[0]
    hown = history.shape[0]
    seq = own * grps
    total = seq + hown * secs
    block = 2 * own
    hist = history.reshape(hown, 2 * HD)
    anywhere = pl.BlockSpec(memory_space=pl.ANY)
    vmem = pl.BlockSpec(memory_space=pltpu.VMEM)
    smem = pl.BlockSpec(memory_space=pltpu.SMEM)
    dma = pltpu.SemaphoreType.DMA
    gq, gk, gv, gh = pl.pallas_call(
        functools.partial(kernel, secs, grps),
        out_shape=[
            jax.ShapeDtypeStruct(queries.shape, BF),
            jax.ShapeDtypeStruct(keys.shape, BF),
            jax.ShapeDtypeStruct(values.shape, BF),
            jax.ShapeDtypeStruct((hown, 2 * HD), F32),
        ],
        in_specs=[anywhere] * 5 + [smem],
        out_specs=[anywhere] * 3 + [vmem],
        scratch_shapes=[
            pltpu.VMEM((seq, HD), BF),
            pltpu.VMEM((seq, HD), BF),
            pltpu.VMEM((total, HD), BF),
            pltpu.VMEM((total, HD), BF),
            pltpu.VMEM((HD, total), BF),
            pltpu.VMEM((total, block), F32),
            pltpu.VMEM((total, block), F32),
            pltpu.VMEM((total, block), F32),
            pltpu.VMEM((total, HD), F32),
            pltpu.VMEM((total, HD), F32),
            pltpu.VMEM((seq, HD), BF),
            pltpu.VMEM((total, HD), BF),
            pltpu.VMEM((total, HD), BF),
            pltpu.VMEM((secs * hown, HD), BF),
            pltpu.VMEM((secs * hown, HD), BF),
            dma((4, grps)),
            dma((4, grps)),
            dma((2, secs)),
            dma((2, secs)),
            dma((3, grps)),
            dma((3, grps)),
            dma((2, secs)),
            dma((2, secs)),
        ],
        compiler_params=pltpu.CompilerParams(
            collective_id=0, has_side_effects=True, vmem_limit_bytes=40 * 2**20
        ),
    )(queries, keys, values, dout, hist, context)
    return gq, gk, gv, gh.reshape(hown, 2, HD)


def solution(mesh):
    secs, grps = mesh.shape["sec"], mesh.shape["grp"]
    split = P(("sec", "grp"), None)
    return jax.shard_map(
        functools.partial(on_device, secs, grps),
        mesh=mesh,
        in_specs=(split, split, split, split, P("sec", None, "grp"), P()),
        out_specs=(split, split, split, P("sec", None, "grp")),
        check_vma=False,
    )
```

time: 364 us -> 105 us (0.29)
  waiting for transfers between devices: 159 us -> 0 us
  Pallas kernels: 0 us -> 95.4 us
  matrix products: 68.1 us -> 0 us
  blocking collectives: 40.8 us -> 0 us
  starting transfers between devices: 34.4 us -> 0 us
  local copies, waits for them, and re-layouts: 35.5 us -> 8.62 us
  between operations: 14.9 us -> 0.65 us
  other arithmetic: 7.01 us -> 0 us
    psum x1 -> x0, waiting for transfers between devices: 95.9 us -> none  [on_device(): total = lax.psum(hist_terms.astype(jnp.bfloat16), 'sec').astype(jnp.float32)]
    pallas_call x0 -> x1, Pallas kernels: none -> 95.4 us  [on_device(): pl.pallas_call(functools.partial(kernel, secs, grps), out_shape=[jax.Shap...]
    dot_general x24 -> x0, matrix products: 68.1 us -> none  [the longest x4 22.2 us: step(): jnp.einsum('hbk,bhd->khd', probs_low, g_block, preferred_element_type=jnp...]
    all_to_all x6 -> x0, waiting for transfers between devices: 63.5 us -> none  [the longest x1 16.9 us: on_device(): lax.all_to_all(grad_k, 'grp', split_axis=0, concat_axis=1, tiled=True)]
    all_to_all x6 -> x0, starting transfers between devices: 34.4 us -> none  [the longest x1 9.98 us: swap_heads(): lax.all_to_all(values, 'grp', split_axis=1, concat_axis=0, tiled=True)]
    all_gather x1 -> x0, blocking collectives: 20.8 us -> none  [fetch_history(): return lax.all_gather(history, 'sec', axis=0, tiled=True)]
    all_to_all x1 -> x0, blocking collectives: 20 us -> none  [on_device(): lax.all_to_all(grad_v, 'grp', split_axis=0, concat_axis=1, tiled=True)]
    while x18 -> x0, local copies, waits for them, and re-layouts: 9.85 us -> none
  transfers between devices with their start and end apart: 7 -> 0, of which waited for: 5 -> 0; matrix products, arithmetic and copies ran while one was open for 4% -> 0% of each run, Pallas kernels for 0% -> 0%
where the time goes in v1:
time: 105 us
  Pallas kernels  95.4 us (91%)
  local copies, waits for them, and re-layouts  8.62 us (8%)
    pallas_call x1, Pallas kernels, on_device(): pl.pallas_call(functools.partial(kernel, secs, grps), out_shape=[jax.Shap...  95.4 us
    unnamed x14, local copies, waits for them, and re-layouts  7.96 us

profile of v1, /device:TPU:1, one launch (start us, length us, event | category | flops | bytes accessed | tf_op | source)
XLA Modules:
  0.0 104.7 jit_solution(47419544093142725)
XLA Ops:
  0.6 0.8 copy.12
  1.4 0.0 copy-start.4
  1.4 0.7 copy-done.4
  2.1 0.0 copy-start
  2.1 1.0 copy-done
  3.1 0.0 copy-start.1
  3.1 1.0 copy-done.1
  4.1 0.0 copy-start.2
  4.1 1.0 copy-done.2
  5.2 0.0 copy-start.3
  5.2 1.0 copy-done.3
  6.2 95.4 %shard_map.93 = (bf16[128,2048]{1,0:T(8,128)(2,1)S(1)}, bf16[128,2048]{1,0:T(8,128)(2,1)S(1)}, bf16[128,2048]{1,0:T(8,128)(2,1)S(1)}, f32[64,256]{1,0:T(8,128)S(1)}) custom-call(bf16[128,2048]{1,0:T(8,128)(2,1)S(1)} %copy-done, bf16[128,2048]{1,0:T(8,128)(2,1)S(1)} %copy-done.1, bf16[128,2048]{1,0:T(8,128)(2,1)S(1)} %copy-done.2, ...), custom_call_target="tpu_custom_call" | custom-call | tf_op jit(solution)/shard_map/pallas_call | solution.py:351
  101.6 0.7 reshape.15
  102.3 0.8 copy.16
  103.1 0.8 copy.17
  103.9 0.8 copy.18
Async XLA Ops:
  1.4 0.7 copy-start.4
  2.1 1.0 copy-start
  3.1 1.0 copy-start.1
  4.1 1.0 copy-start.2
  5.2 1.0 copy-start.3

commit v2 on v1

--- a/solution.py
+++ b/solution.py
@@ -17,6 +17,7 @@
 SCALE = HD ** (-0.5)
 LOG2E = math.log2(math.e)
 KC = 512
+VLIM = 58
 
 
 def dot(a, b, dims=NN):
@@ -49,8 +50,10 @@
     dqs,
     dks,
     dvs,
-    hbk,
-    hbv,
+    hb,
+    hf,
+    hgs,
+    hgr,
     in_send,
     in_recv,
     h_send,
@@ -59,12 +62,14 @@
     out_recv,
     gh_send,
     gh_recv,
+    line_sem,
+    go_sem,
 ):
     own = q_in.shape[0]
     chips = grps // 2
     block = 2 * own
     seq = grps * own
-    hown = h_in.shape[0]
+    hown = h_in.shape[0] // 2
     keys = seq + secs * hown
     parts = keys // KC
     sec = lax.axis_index("sec")
@@ -88,22 +93,6 @@
 
     def rows(d, n, base=0):
         return pl.ds(pl.multiple_of(base + d * n, n), n)
-
-    barrier = pltpu.get_barrier_semaphore()
-
-    @pl.loop(1, grps)
-    def _(i):
-        pl.semaphore_signal(
-            barrier, 1, device_id=(sec, (grp + i) % grps), device_id_type=MESH
-        )
-
-    @pl.loop(1, secs)
-    def _(i):
-        pl.semaphore_signal(
-            barrier, 1, device_id=((sec + i) % secs, grp), device_id_type=MESH
-        )
-
-    pl.semaphore_wait(barrier, grps + secs - 2)
 
     def in_copy(a, src, dst, t, dc):
         to = device(to_chip(t), dc)
@@ -123,24 +112,68 @@
 
     arrays = ((0, k_in, kb), (1, v_in, vb), (2, q_in, qb), (3, g_in, gb))
 
-    def h_copy(a, dst, i):
+    def h_copy(i):
         return pltpu.make_async_remote_copy(
-            h_in.at[:, pl.ds(a * HD, HD)],
-            dst.at[rows(sec, hown, seq)],
-            h_send.at[a, i],
-            h_recv.at[a, i],
+            h_in,
+            hb.at[rows(sec, 2 * hown)],
+            h_send.at[i],
+            h_recv.at[i],
             device_id=((sec + i) % secs, grp),
             device_id_type=MESH,
         )
 
-    def h_local(a, dst):
-        return pltpu.make_async_copy(
-            h_in.at[:, pl.ds(a * HD, HD)], dst.at[rows(sec, hown, seq)], h_recv.at[a, 0]
-        )
+    h_local = pltpu.make_async_copy(h_in, hb.at[rows(sec, 2 * hown)], h_recv.at[0])
+
+    for a, src, dst in arrays:
+        in_local(a, src, dst).start()
+    h_local.start()
+
+    beside = 2 * (chips // 2 + 1)
+    leader = beside + 1
+    barrier = pltpu.get_barrier_semaphore()
+
+    @pl.loop(1, grps)
+    def _(i):
+        to = (grp + i) % grps
+
+        @pl.when(to != leader)
+        def _():
+            pl.semaphore_signal(barrier, 1, device_id=(sec, to), device_id_type=MESH)
+
+    @pl.when(grp != leader)
+    def _():
+        pl.semaphore_wait(barrier, grps - 1)
+
+    @pl.when(grp == beside)
+    def _():
+        pl.semaphore_signal(line_sem, 1, device_id=(sec, leader), device_id_type=MESH)
+
+    @pl.when(grp == leader)
+    def _():
+        pl.semaphore_wait(line_sem, 1)
+
+        @pl.loop(1, secs)
+        def _(i):
+            pl.semaphore_signal(
+                barrier, 1, device_id=((sec + i) % secs, grp), device_id_type=MESH
+            )
+
+    def all_there():
+        @pl.when(grp == leader)
+        def _():
+            pl.semaphore_wait(barrier, secs - 1)
+
+            @pl.loop(1, grps)
+            def _(i):
+                pl.semaphore_signal(
+                    go_sem, 1, device_id=(sec, (grp + i) % grps), device_id_type=MESH
+                )
+
+        @pl.when(grp != leader)
+        def _():
+            pl.semaphore_wait(go_sem, 1)
 
     def start_in(first, last):
-        for a, src, dst in arrays[first:last]:
-            in_local(a, src, dst).start()
         for a, src, dst in arrays[first:last]:
             in_copy(a, src, dst, 0, 1).start()
 
@@ -150,15 +183,14 @@
                 in_copy(a, src, dst, t, 0).start()
                 in_copy(a, src, dst, t, 1).start()
 
-    start_in(0, 2)
-    for a, dst in ((0, kb), (1, vb)):
-        h_local(a, dst).start()
+    start_in(0, 1)
+    all_there()
 
     @pl.loop(1, secs)
     def _(i):
-        h_copy(0, kb, i).start()
-        h_copy(1, vb, i).start()
-
+        h_copy(i).start()
+
+    start_in(1, 2)
     start_in(2, 4)
 
     dka[...] = jnp.zeros_like(dka)
@@ -178,19 +210,22 @@
         else:
             in_copy(a, src, dst, t, dc).wait_recv()
 
+    h_local.wait()
+
+    @pl.loop(1, secs)
+    def _(i):
+        h_copy(i).wait_recv()
+
+    hist = secs * hown
+    hf[...] = hb[...].astype(F32)
+    kb[seq:, :] = hf[pl.ds(0, hist, stride=2), :].astype(BF)
+    vb[seq:, :] = hf[pl.ds(1, hist, stride=2), :].astype(BF)
+
     @pl.loop(0, chips)
     def _(t):
         for a, src, dst in arrays[:2]:
             for dc in range(2):
                 wait_in(a, src, dst, t, dc)
-
-    for a, dst in ((0, kb), (1, vb)):
-        h_local(a, dst).wait()
-
-    @pl.loop(1, secs)
-    def _(i):
-        h_copy(0, kb, i).wait_recv()
-        h_copy(1, vb, i).wait_recv()
 
     for j in range(parts):
         kt[:, j * KC : (j + 1) * KC] = kb[j * KC : (j + 1) * KC, :].T
@@ -264,34 +299,33 @@
             dka[part, :] += dot(ds, qs)
             dqt = dqt + dot(kt[:, part], ds)
         dqs[here, :] = jnp.transpose(dqt * (inv * SCALE)).astype(BF)
+
         start_out(0, dqs, gq_out, t)
 
-    def gh_copy(a, src, dst, i):
+    def gh_copy(i):
         to = (sec + i) % secs
         return pltpu.make_async_remote_copy(
-            src.at[rows(to, hown, seq)],
-            dst.at[rows(i, hown)],
-            gh_send.at[a, i],
-            gh_recv.at[a, i],
+            hgs.at[rows(to, 2 * hown)],
+            hgr.at[rows(i, 2 * hown)],
+            gh_send.at[i],
+            gh_recv.at[i],
             device_id=(to, grp),
             device_id_type=MESH,
         )
 
-    def gh_local(a, src, dst):
-        return pltpu.make_async_copy(
-            src.at[rows(sec, hown, seq)], dst.at[rows(0, hown)], gh_recv.at[a, 0]
-        )
-
-    hist_parts = ((0, dks, hbk), (1, dvs, hbv))
-    dks[seq:, :] = dka[seq:, :].astype(BF)
-    dvs[seq:, :] = dva[seq:, :].astype(BF)
-    for a, src, dst in hist_parts:
-        gh_local(a, src, dst).start()
+    gh_local = pltpu.make_async_copy(
+        hgs.at[rows(sec, 2 * hown)], hgr.at[rows(0, 2 * hown)], gh_recv.at[0]
+    )
+
+    for i in range(secs):
+        mine = slice(seq + i * hown, seq + (i + 1) * hown)
+        hgs[2 * i * hown : (2 * i + 1) * hown, :] = dka[mine, :].astype(BF)
+        hgs[(2 * i + 1) * hown : (2 * i + 2) * hown, :] = dva[mine, :].astype(BF)
+    gh_local.start()
 
     @pl.loop(1, secs)
     def _(i):
-        for a, src, dst in hist_parts:
-            gh_copy(a, src, dst, i).start()
+        gh_copy(i).start()
 
     back = ((1, dks, gk_out), (2, dvs, gv_out))
 
@@ -303,24 +337,21 @@
         for a, src, dst in back:
             start_out(a, src, dst, t)
 
-    for a, src, dst in hist_parts:
-        gh_local(a, src, dst).wait()
+    gh_local.wait()
 
     @pl.loop(1, secs)
     def _(i):
-        for a, src, dst in hist_parts:
-            gh_copy(a, src, dst, i).wait()
-
-    for a, buf in ((0, hbk), (1, hbv)):
-        acc = buf[0:hown, :].astype(F32)
-        for i in range(1, secs):
-            acc = acc + buf[i * hown : (i + 1) * hown, :].astype(F32)
-        gh_out[:, a * HD : (a + 1) * HD] = acc
+        gh_copy(i).wait()
+
+    acc = hgr[0 : 2 * hown, :].astype(F32)
+    for i in range(1, secs):
+        acc = acc + hgr[2 * i * hown : 2 * (i + 1) * hown, :].astype(F32)
+    gh_out[pl.ds(0, hown, stride=2), :] = acc[:hown, :]
+    gh_out[pl.ds(1, hown, stride=2), :] = acc[hown:, :]
 
     @pl.loop(1, secs)
     def _(i):
-        h_copy(0, kb, i).wait_send()
-        h_copy(1, vb, i).wait_send()
+        h_copy(i).wait_send()
 
     for a, src, dst in arrays:
         in_copy(a, src, dst, 0, 1).wait_send()
@@ -337,13 +368,40 @@
                 out_copy(a, src, dst, t, dc).wait()
 
 
+def settle_kernel(n, *refs):
+    ins, outs, held, sem = refs[:n], refs[n : 2 * n], refs[2 * n : 3 * n], refs[3 * n]
+    arrive = [pltpu.make_async_copy(ins[i], held[i], sem.at[i]) for i in range(n)]
+    leave = [pltpu.make_async_copy(held[i], outs[i], sem.at[n + i]) for i in range(n)]
+    for copy in arrive:
+        copy.start()
+    for i in range(n):
+        arrive[i].wait()
+        leave[i].start()
+    for copy in leave:
+        copy.wait()
+
+
+def settle(*arrays):
+    n = len(arrays)
+    anywhere = pl.BlockSpec(memory_space=pl.ANY)
+    return pl.pallas_call(
+        functools.partial(settle_kernel, n),
+        out_shape=[jax.ShapeDtypeStruct(a.shape, a.dtype) for a in arrays],
+        in_specs=[anywhere] * n,
+        out_specs=[anywhere] * n,
+        scratch_shapes=[pltpu.VMEM(a.shape, a.dtype) for a in arrays]
+        + [pltpu.SemaphoreType.DMA((2 * n,))],
+        compiler_params=pltpu.CompilerParams(vmem_limit_bytes=VLIM * 2**20),
+    )(*arrays)
+
+
 def on_device(secs, grps, queries, keys, values, dout, history, context):
     own = queries.shape[0]
     hown = history.shape[0]
     seq = own * grps
     total = seq + hown * secs
     block = 2 * own
-    hist = history.reshape(hown, 2 * HD)
+    hist = history.reshape(2 * hown, HD)
     anywhere = pl.BlockSpec(memory_space=pl.ANY)
     vmem = pl.BlockSpec(memory_space=pltpu.VMEM)
     smem = pl.BlockSpec(memory_space=pltpu.SMEM)
@@ -354,7 +412,7 @@
             jax.ShapeDtypeStruct(queries.shape, BF),
             jax.ShapeDtypeStruct(keys.shape, BF),
             jax.ShapeDtypeStruct(values.shape, BF),
-            jax.ShapeDtypeStruct((hown, 2 * HD), F32),
+            jax.ShapeDtypeStruct((2 * hown, HD), F32),
         ],
         in_specs=[anywhere] * 5 + [smem],
         out_specs=[anywhere] * 3 + [vmem],
@@ -370,23 +428,28 @@
             pltpu.VMEM((total, HD), F32),
             pltpu.VMEM((total, HD), F32),
             pltpu.VMEM((seq, HD), BF),
-            pltpu.VMEM((total, HD), BF),
-            pltpu.VMEM((total, HD), BF),
-            pltpu.VMEM((secs * hown, HD), BF),
-            pltpu.VMEM((secs * hown, HD), BF),
+            pltpu.VMEM((seq, HD), BF),
+            pltpu.VMEM((seq, HD), BF),
+            pltpu.VMEM((2 * secs * hown, HD), BF),
+            pltpu.VMEM((2 * secs * hown, HD), F32),
+            pltpu.VMEM((2 * secs * hown, HD), BF),
+            pltpu.VMEM((2 * secs * hown, HD), BF),
             dma((4, grps)),
             dma((4, grps)),
-            dma((2, secs)),
-            dma((2, secs)),
+            dma((secs,)),
+            dma((secs,)),
             dma((3, grps)),
             dma((3, grps)),
-            dma((2, secs)),
-            dma((2, secs)),
+            dma((secs,)),
+            dma((secs,)),
+            pltpu.SemaphoreType.REGULAR,
+            pltpu.SemaphoreType.REGULAR,
         ],
         compiler_params=pltpu.CompilerParams(
-            collective_id=0, has_side_effects=True, vmem_limit_bytes=40 * 2**20
+            collective_id=0, has_side_effects=True, vmem_limit_bytes=VLIM * 2**20
         ),
     )(queries, keys, values, dout, hist, context)
+    gq, gk, gv, gh = settle(gq, gk, gv, gh)
     return gq, gk, gv, gh.reshape(hown, 2, HD)
 
 

time: 105 us -> 97.4 us (0.928)
  local copies, waits for them, and re-layouts: 8.62 us -> 0 us
  Pallas kernels: 95.4 us -> 96.6 us
    unnamed x14 -> x0, local copies, waits for them, and re-layouts: 7.96 us -> none
    pallas_call x0 -> x1, Pallas kernels: none -> 2.26 us  [settle(): pl.pallas_call(functools.partial(settle_kernel, n), out_shape=[jax.ShapeD...]
where the time goes in v2:
time: 97.4 us; the launch traced here: 97.2 us
  Pallas kernels  96.6 us (99%)
    pallas_call x1, Pallas kernels, on_device(): pl.pallas_call(functools.partial(kernel, secs, grps), out_shape=[jax.Shap...  94.3 us
    pallas_call x1, Pallas kernels, settle(): pl.pallas_call(functools.partial(settle_kernel, n), out_shape=[jax.ShapeD...  2.26 us

profile of v2, /device:TPU:1, one launch (start us, length us, event | category | flops | bytes accessed | tf_op | source)
XLA Modules:
  0.0 97.2 jit_solution(9642309826382625782)
XLA Ops:
  0.6 94.3 %shard_map.93 = (bf16[128,2048]{1,0:T(8,128)(2,1)}, bf16[128,2048]{1,0:T(8,128)(2,1)}, bf16[128,2048]{1,0:T(8,128)(2,1)}, f32[128,128]{1,0:T(8,128)}) custom-call(bf16[128,2048]{1,0:T(8,128)(2,1)} %q_in.1, bf16[128,2048]{1,0:T(8,128)(2,1)} %k_in.1, bf16[128,2048]{1,0:T(8,128)(2,1)} %v_in.1, bf16[128,2048]{1,0:T(8,128)(2,1)} %g_in.1, ...), custom_call_target="tpu_custom_call" | custom-call | tf_op jit(solution)/shard_map/pallas_call | solution.py:409
  95.0 2.3 %shard_map.94 = (bf16[128,2048]{1,0:T(8,128)(2,1)}, bf16[128,2048]{1,0:T(8,128)(2,1)}, bf16[128,2048]{1,0:T(8,128)(2,1)}, f32[128,128]{1,0:T(8,128)}) custom-call(bf16[128,2048]{1,0:T(8,128)(2,1)} %get-tuple-element.12.refs_0_, bf16[128,2048]{1,0:T(8,128)(2,1)} %get-tuple-element.13.refs_1_, bf16[128,2048]{1,0:T(8,128)(2,1)} %get-tuple-element.14.refs_2_, ...), custom_call_target="tpu_custom_call" | custom-call | tf_op jit(solution)/shard_map/pallas_call | solution.py:387

commit v3 on v2

--- a/solution.py
+++ b/solution.py
@@ -16,7 +16,7 @@
 BF = jnp.bfloat16
 SCALE = HD ** (-0.5)
 LOG2E = math.log2(math.e)
-KC = 512
+KC = 256
 VLIM = 58
 
 
@@ -64,6 +64,9 @@
     gh_recv,
     line_sem,
     go_sem,
+    ctx_all,
+    ghs,
+    own_sem,
 ):
     own = q_in.shape[0]
     chips = grps // 2
@@ -79,6 +82,9 @@
     def shift(t):
         return ((t + 1) // 2) * (2 * (t % 2) - 1) + chips
 
+    def turn(i):
+        return i + ((i + 13) // 16) * (10 - 2 * i)
+
     def to_chip(t):
         return (z + shift(t)) % chips
 
@@ -124,21 +130,26 @@
 
     h_local = pltpu.make_async_copy(h_in, hb.at[rows(sec, 2 * hown)], h_recv.at[0])
 
+    beside = 2 * (chips // 2 + 1)
+    leader = beside + 1
+    barrier = pltpu.get_barrier_semaphore()
+    for t in reversed(range(chips)):
+        for dc in range(2):
+            if t or dc:
+                to = device(to_chip(t), dc)
+
+                @pl.when(to != leader)
+                def _(to=to):
+                    pl.semaphore_signal(
+                        barrier, 1, device_id=(sec, to), device_id_type=MESH
+                    )
+
     for a, src, dst in arrays:
         in_local(a, src, dst).start()
     h_local.start()
-
-    beside = 2 * (chips // 2 + 1)
-    leader = beside + 1
-    barrier = pltpu.get_barrier_semaphore()
-
-    @pl.loop(1, grps)
-    def _(i):
-        to = (grp + i) % grps
-
-        @pl.when(to != leader)
-        def _():
-            pl.semaphore_signal(barrier, 1, device_id=(sec, to), device_id_type=MESH)
+    ctx_copy = pltpu.make_async_copy(ctx_in, ctx_all, own_sem.at[0])
+    ctx_copy.start()
+    gh_copy_out = pltpu.make_async_copy(ghs, gh_out, own_sem.at[1])
 
     @pl.when(grp != leader)
     def _():
@@ -178,7 +189,8 @@
             in_copy(a, src, dst, 0, 1).start()
 
         @pl.loop(1, chips)
-        def _(t):
+        def _(i):
+            t = turn(i)
             for a, src, dst in arrays[first:last]:
                 in_copy(a, src, dst, t, 0).start()
                 in_copy(a, src, dst, t, 1).start()
@@ -195,7 +207,6 @@
 
     dka[...] = jnp.zeros_like(dka)
     dva[...] = jnp.zeros_like(dva)
-    ctx = ctx_in[sec]
 
     def wait_in(a, src, dst, t, dc):
         if dc == 0:
@@ -211,6 +222,8 @@
             in_copy(a, src, dst, t, dc).wait_recv()
 
     h_local.wait()
+    ctx_copy.wait()
+    ctx = ctx_all[sec]
 
     @pl.loop(1, secs)
     def _(i):
@@ -258,7 +271,8 @@
             out_copy(a, src, dst, t, 0).start()
 
     @pl.loop(0, chips)
-    def _(t):
+    def _(i):
+        t = turn(i)
         for a, src, dst in arrays[2:]:
             for dc in range(2):
                 wait_in(a, src, dst, t, dc)
@@ -330,7 +344,8 @@
     back = ((1, dks, gk_out), (2, dvs, gv_out))
 
     @pl.loop(0, chips)
-    def _(t):
+    def _(i):
+        t = chips - 1 - i
         here = rows(from_chip(t), block)
         dks[here, :] = dka[here, :].astype(BF)
         dvs[here, :] = dva[here, :].astype(BF)
@@ -346,8 +361,11 @@
     acc = hgr[0 : 2 * hown, :].astype(F32)
     for i in range(1, secs):
         acc = acc + hgr[2 * i * hown : 2 * (i + 1) * hown, :].astype(F32)
-    gh_out[pl.ds(0, hown, stride=2), :] = acc[:hown, :]
-    gh_out[pl.ds(1, hown, stride=2), :] = acc[hown:, :]
+    ghs[pl.ds(0, hown, stride=2), :] = acc[:hown, :]
+    ghs[pl.ds(1, hown, stride=2), :] = acc[hown:, :]
+    gh_copy_out.start()
+
+    gh_copy_out.wait()
 
     @pl.loop(1, secs)
     def _(i):
@@ -355,17 +373,26 @@
 
     for a, src, dst in arrays:
         in_copy(a, src, dst, 0, 1).wait_send()
-    for a, src, dst in ((0, dqs, gq_out),) + back:
-        out_copy(a, src, dst, 0, 1).wait()
-        out_local(a, src, dst).wait()
+    out_copy(0, dqs, gq_out, 0, 1).wait()
+    out_local(0, dqs, gq_out).wait()
 
     @pl.loop(1, chips)
-    def _(t):
+    def _(i):
+        t = turn(i)
         for dc in range(2):
             for a, src, dst in arrays:
                 in_copy(a, src, dst, t, dc).wait_send()
-            for a, src, dst in ((0, dqs, gq_out),) + back:
-                out_copy(a, src, dst, t, dc).wait()
+            out_copy(0, dqs, gq_out, t, dc).wait()
+
+    @pl.loop(1, chips)
+    def _(i):
+        for a, src, dst in back:
+            for dc in range(2):
+                out_copy(a, src, dst, chips - i, dc).wait()
+
+    for a, src, dst in back:
+        out_copy(a, src, dst, 0, 1).wait()
+        out_local(a, src, dst).wait()
 
 
 def settle_kernel(n, *refs):
@@ -403,8 +430,6 @@
     block = 2 * own
     hist = history.reshape(2 * hown, HD)
     anywhere = pl.BlockSpec(memory_space=pl.ANY)
-    vmem = pl.BlockSpec(memory_space=pltpu.VMEM)
-    smem = pl.BlockSpec(memory_space=pltpu.SMEM)
     dma = pltpu.SemaphoreType.DMA
     gq, gk, gv, gh = pl.pallas_call(
         functools.partial(kernel, secs, grps),
@@ -414,8 +439,8 @@
             jax.ShapeDtypeStruct(values.shape, BF),
             jax.ShapeDtypeStruct((2 * hown, HD), F32),
         ],
-        in_specs=[anywhere] * 5 + [smem],
-        out_specs=[anywhere] * 3 + [vmem],
+        in_specs=[anywhere] * 6,
+        out_specs=[anywhere] * 4,
         scratch_shapes=[
             pltpu.VMEM((seq, HD), BF),
             pltpu.VMEM((seq, HD), BF),
@@ -444,6 +469,9 @@
             dma((secs,)),
             pltpu.SemaphoreType.REGULAR,
             pltpu.SemaphoreType.REGULAR,
+            pltpu.SMEM((secs,), jnp.int32),
+            pltpu.VMEM((2 * hown, HD), F32),
+            dma((2,)),
         ],
         compiler_params=pltpu.CompilerParams(
             collective_id=0, has_side_effects=True, vmem_limit_bytes=VLIM * 2**20

time: 97.4 us -> 94.9 us (0.974)
  Pallas kernels: 96.6 us -> 94.1 us
    pallas_call x1, Pallas kernels: 94.3 us -> 91.9 us  [on_device(): pl.pallas_call(functools.partial(kernel, secs, grps), out_shape=[jax.Shap...]
where the time goes in v3:
time: 94.9 us; the launch traced here: 94.8 us
  Pallas kernels  94.1 us (99%)
    pallas_call x1, Pallas kernels, on_device(): pl.pallas_call(functools.partial(kernel, secs, grps), out_shape=[jax.Shap...  91.9 us
    pallas_call x1, Pallas kernels, settle(): pl.pallas_call(functools.partial(settle_kernel, n), out_shape=[jax.ShapeD...  2.26 us

profile of v3, /device:TPU:1, one launch (start us, length us, event | category | flops | bytes accessed | tf_op | source)
XLA Modules:
  0.0 94.8 jit_solution(9057847755907798454)
XLA Ops:
  0.6 91.9 %shard_map.93 = (bf16[128,2048]{1,0:T(8,128)(2,1)}, bf16[128,2048]{1,0:T(8,128)(2,1)}, bf16[128,2048]{1,0:T(8,128)(2,1)}, f32[128,128]{1,0:T(8,128)}) custom-call(bf16[128,2048]{1,0:T(8,128)(2,1)} %q_in.1, bf16[128,2048]{1,0:T(8,128)(2,1)} %k_in.1, bf16[128,2048]{1,0:T(8,128)(2,1)} %v_in.1, bf16[128,2048]{1,0:T(8,128)(2,1)} %g_in.1, ...), custom_call_target="tpu_custom_call" | custom-call | tf_op jit(solution)/shard_map/pallas_call | solution.py:434
  92.5 2.3 %shard_map.94 = (bf16[128,2048]{1,0:T(8,128)(2,1)}, bf16[128,2048]{1,0:T(8,128)(2,1)}, bf16[128,2048]{1,0:T(8,128)(2,1)}, f32[128,128]{1,0:T(8,128)}) custom-call(bf16[128,2048]{1,0:T(8,128)(2,1)} %get-tuple-element.12.refs_0_, bf16[128,2048]{1,0:T(8,128)(2,1)} %get-tuple-element.13.refs_1_, bf16[128,2048]{1,0:T(8,128)(2,1)} %get-tuple-element.14.refs_2_, ...), custom_call_target="tpu_custom_call" | custom-call | tf_op jit(solution)/shard_map/pallas_call | solution.py:414

commit v4 on v3

--- a/solution.py
+++ b/solution.py
@@ -17,7 +17,7 @@
 SCALE = HD ** (-0.5)
 LOG2E = math.log2(math.e)
 KC = 256
-VLIM = 58
+VLIM = 48
 
 
 def dot(a, b, dims=NN):
@@ -396,15 +396,11 @@
 
 
 def settle_kernel(n, *refs):
-    ins, outs, held, sem = refs[:n], refs[n : 2 * n], refs[2 * n : 3 * n], refs[3 * n]
-    arrive = [pltpu.make_async_copy(ins[i], held[i], sem.at[i]) for i in range(n)]
-    leave = [pltpu.make_async_copy(held[i], outs[i], sem.at[n + i]) for i in range(n)]
-    for copy in arrive:
+    ins, outs, sem = refs[:n], refs[n : 2 * n], refs[2 * n]
+    copies = [pltpu.make_async_copy(ins[i], outs[i], sem.at[i]) for i in range(n)]
+    for copy in copies:
         copy.start()
-    for i in range(n):
-        arrive[i].wait()
-        leave[i].start()
-    for copy in leave:
+    for copy in copies:
         copy.wait()
 
 
@@ -416,10 +412,9 @@
         out_shape=[jax.ShapeDtypeStruct(a.shape, a.dtype) for a in arrays],
         in_specs=[anywhere] * n,
         out_specs=[anywhere] * n,
-        scratch_shapes=[pltpu.VMEM(a.shape, a.dtype) for a in arrays]
-        + [pltpu.SemaphoreType.DMA((2 * n,))],
-        compiler_params=pltpu.CompilerParams(vmem_limit_bytes=VLIM * 2**20),
-    )(*arrays)
+        scratch_shapes=[pltpu.SemaphoreType.DMA((n,))],
+        compiler_params=pltpu.CompilerParams(vmem_limit_bytes=8 * 2**20),
+    )(*[pltpu.with_memory_space_constraint(a, pltpu.VMEM) for a in arrays])
 
 
 def on_device(secs, grps, queries, keys, values, dout, history, context):
@@ -431,16 +426,17 @@
     hist = history.reshape(2 * hown, HD)
     anywhere = pl.BlockSpec(memory_space=pl.ANY)
     dma = pltpu.SemaphoreType.DMA
+    args = (queries, keys, values, dout, hist, context)
     gq, gk, gv, gh = pl.pallas_call(
         functools.partial(kernel, secs, grps),
         out_shape=[
-            jax.ShapeDtypeStruct(queries.shape, BF),
-            jax.ShapeDtypeStruct(keys.shape, BF),
-            jax.ShapeDtypeStruct(values.shape, BF),
-            jax.ShapeDtypeStruct((2 * hown, HD), F32),
+            pltpu.VMEM(queries.shape, BF),
+            pltpu.VMEM(keys.shape, BF),
+            pltpu.VMEM(values.shape, BF),
+            pltpu.VMEM((2 * hown, HD), F32),
         ],
         in_specs=[anywhere] * 6,
-        out_specs=[anywhere] * 4,
+        out_specs=[pl.BlockSpec(memory_space=pltpu.VMEM)] * 4,
         scratch_shapes=[
             pltpu.VMEM((seq, HD), BF),
             pltpu.VMEM((seq, HD), BF),
@@ -476,7 +472,7 @@
         compiler_params=pltpu.CompilerParams(
             collective_id=0, has_side_effects=True, vmem_limit_bytes=VLIM * 2**20
         ),
-    )(queries, keys, values, dout, hist, context)
+    )(*[pltpu.with_memory_space_constraint(a, pltpu.HBM) for a in args])
     gq, gk, gv, gh = settle(gq, gk, gv, gh)
     return gq, gk, gv, gh.reshape(hown, 2, HD)
 

time: 94.9 us -> 93.7 us (0.987)
  Pallas kernels: 94.1 us -> 93 us
    pallas_call x1, Pallas kernels: 2.26 us -> 1.18 us  [settle(): pl.pallas_call(functools.partial(settle_kernel, n), out_shape=[jax.ShapeD...]
where the time goes in v4:
time: 93.7 us; the launch traced here: 93.6 us
  Pallas kernels  93 us (99%)
    pallas_call x1, Pallas kernels, on_device(): pl.pallas_call(functools.partial(kernel, secs, grps), out_shape=[pltpu.VM...  91.8 us

profile of v4, /device:TPU:1, one launch (start us, length us, event | category | flops | bytes accessed | tf_op | source)
XLA Modules:
  0.0 93.6 jit_solution(10239019885015549831)
XLA Ops:
  0.6 91.8 %shard_map.93 = (bf16[128,2048]{1,0:T(8,128)(2,1)S(1)}, bf16[128,2048]{1,0:T(8,128)(2,1)S(1)}, bf16[128,2048]{1,0:T(8,128)(2,1)S(1)}, f32[128,128]{1,0:T(8,128)S(1)}) custom-call(bf16[128,2048]{1,0:T(8,128)(2,1)} %q_in.1, bf16[128,2048]{1,0:T(8,128)(2,1)} %k_in.1, bf16[128,2048]{1,0:T(8,128)(2,1)} %v_in.1, bf16[128,2048]{1,0:T(8,128)(2,1)} %g_in.1, ...), custom_call_target="tpu_custom_call" | custom-call | tf_op jit(solution)/shard_map/pallas_call | solution.py:430
  92.4 1.2 %shard_map.94 = (bf16[128,2048]{1,0:T(8,128)(2,1)}, bf16[128,2048]{1,0:T(8,128)(2,1)}, bf16[128,2048]{1,0:T(8,128)(2,1)}, f32[128,128]{1,0:T(8,128)}) custom-call(bf16[128,2048]{1,0:T(8,128)(2,1)S(1)} %get-tuple-element.12.refs_0_, bf16[128,2048]{1,0:T(8,128)(2,1)S(1)} %get-tuple-element.13.refs_1_, bf16[128,2048]{1,0:T(8,128)(2,1)S(1)} %get-tuple-element.14.refs_2_, ...), custom_call_target="tpu_custom_call" | custom-call | tf_op jit(solution)/shard_map/pallas_call | solution.py:410

commit v5 on v4

--- a/solution.py
+++ b/solution.py
@@ -64,6 +64,7 @@
     gh_recv,
     line_sem,
     go_sem,
+    near_sem,
     ctx_all,
     ghs,
     own_sem,
@@ -133,16 +134,12 @@
     beside = 2 * (chips // 2 + 1)
     leader = beside + 1
     barrier = pltpu.get_barrier_semaphore()
-    for t in reversed(range(chips)):
-        for dc in range(2):
-            if t or dc:
-                to = device(to_chip(t), dc)
-
-                @pl.when(to != leader)
-                def _(to=to):
-                    pl.semaphore_signal(
-                        barrier, 1, device_id=(sec, to), device_id_type=MESH
-                    )
+    for t, dc in ((0, 1), (1, 0), (1, 1), (2, 0), (2, 1)):
+        to = device(to_chip(t), dc)
+
+        @pl.when(to != leader)
+        def _(to=to):
+            pl.semaphore_signal(barrier, 1, device_id=(sec, to), device_id_type=MESH)
 
     for a, src, dst in arrays:
         in_local(a, src, dst).start()
@@ -153,7 +150,7 @@
 
     @pl.when(grp != leader)
     def _():
-        pl.semaphore_wait(barrier, grps - 1)
+        pl.semaphore_wait(barrier, 5)
 
     @pl.when(grp == beside)
     def _():
@@ -163,11 +160,26 @@
     def _():
         pl.semaphore_wait(line_sem, 1)
 
-        @pl.loop(1, secs)
-        def _(i):
+    def tell(r):
+        for t in (1, 2):
             pl.semaphore_signal(
-                barrier, 1, device_id=((sec + i) % secs, grp), device_id_type=MESH
+                near_sem.at[r],
+                1,
+                device_id=(sec, device(to_chip(t), 0)),
+                device_id_type=MESH,
             )
+
+    def hear(r):
+        pl.semaphore_wait(near_sem.at[r], 2)
+
+    def meet():
+        @pl.when(grp == leader)
+        def _():
+            @pl.loop(1, secs)
+            def _(i):
+                pl.semaphore_signal(
+                    barrier, 1, device_id=((sec + i) % secs, grp), device_id_type=MESH
+                )
 
     def all_there():
         @pl.when(grp == leader)
@@ -195,14 +207,26 @@
                 in_copy(a, src, dst, t, 0).start()
                 in_copy(a, src, dst, t, 1).start()
 
-    start_in(0, 1)
+    tell(0)
+    for a, src, dst in arrays[:2]:
+        in_copy(a, src, dst, 0, 1).start()
+    for step in range(chips // 2):
+        for t in (2 * step + 1, 2 * step + 2):
+            if t < chips:
+                for a, src, dst in arrays[:2]:
+                    in_copy(a, src, dst, t, 0).start()
+                    in_copy(a, src, dst, t, 1).start()
+        if step < chips // 2 - 1:
+            hear(step)
+            if step < chips // 2 - 2:
+                tell(step + 1)
+    meet()
     all_there()
 
     @pl.loop(1, secs)
     def _(i):
         h_copy(i).start()
 
-    start_in(1, 2)
     start_in(2, 4)
 
     dka[...] = jnp.zeros_like(dka)
@@ -465,6 +489,7 @@
             dma((secs,)),
             pltpu.SemaphoreType.REGULAR,
             pltpu.SemaphoreType.REGULAR,
+            pltpu.SemaphoreType.REGULAR((grps // 4 - 1,)),
             pltpu.SMEM((secs,), jnp.int32),
             pltpu.VMEM((2 * hown, HD), F32),
             dma((2,)),

time: 93.7 us -> 94.8 us (1.012)
  Pallas kernels: 93 us -> 94.1 us
    pallas_call x1, Pallas kernels: 91.8 us -> 92.9 us  [on_device(): pl.pallas_call(functools.partial(kernel, secs, grps), out_shape=[pltpu.VM...]
where the time goes in v5:
time: 94.8 us; the launch traced here: 94.7 us
  Pallas kernels  94.1 us (99%)
    pallas_call x1, Pallas kernels, on_device(): pl.pallas_call(functools.partial(kernel, secs, grps), out_shape=[pltpu.VM...  92.9 us

profile of v5, /device:TPU:1, one launch (start us, length us, event | category | flops | bytes accessed | tf_op | source)
XLA Modules:
  0.0 94.7 jit_solution(9343218118165326249)
XLA Ops:
  0.6 92.9 %shard_map.93 = (bf16[128,2048]{1,0:T(8,128)(2,1)S(1)}, bf16[128,2048]{1,0:T(8,128)(2,1)S(1)}, bf16[128,2048]{1,0:T(8,128)(2,1)S(1)}, f32[128,128]{1,0:T(8,128)S(1)}) custom-call(bf16[128,2048]{1,0:T(8,128)(2,1)} %q_in.1, bf16[128,2048]{1,0:T(8,128)(2,1)} %k_in.1, bf16[128,2048]{1,0:T(8,128)(2,1)} %v_in.1, bf16[128,2048]{1,0:T(8,128)(2,1)} %g_in.1, ...), custom_call_target="tpu_custom_call" | custom-call | tf_op jit(solution)/shard_map/pallas_call | solution.py:454
  93.5 1.2 %shard_map.94 = (bf16[128,2048]{1,0:T(8,128)(2,1)}, bf16[128,2048]{1,0:T(8,128)(2,1)}, bf16[128,2048]{1,0:T(8,128)(2,1)}, f32[128,128]{1,0:T(8,128)}) custom-call(bf16[128,2048]{1,0:T(8,128)(2,1)S(1)} %get-tuple-element.12.refs_0_, bf16[128,2048]{1,0:T(8,128)(2,1)S(1)} %get-tuple-element.13.refs_1_, bf16[128,2048]{1,0:T(8,128)(2,1)S(1)} %get-tuple-element.14.refs_2_, ...), custom_call_target="tpu_custom_call" | custom-call | tf_op jit(solution)/shard_map/pallas_call | solution.py:434

commit v6 on v4

--- a/solution.py
+++ b/solution.py
@@ -234,14 +234,22 @@
     kb[seq:, :] = hf[pl.ds(0, hist, stride=2), :].astype(BF)
     vb[seq:, :] = hf[pl.ds(1, hist, stride=2), :].astype(BF)
 
+    for j in range(seq, keys, KC):
+        kt[:, j : j + KC] = kb[j : j + KC, :].T
+
     @pl.loop(0, chips)
-    def _(t):
-        for a, src, dst in arrays[:2]:
-            for dc in range(2):
-                wait_in(a, src, dst, t, dc)
-
-    for j in range(parts):
-        kt[:, j * KC : (j + 1) * KC] = kb[j * KC : (j + 1) * KC, :].T
+    def _(i):
+        t = turn(i)
+        for dc in range(2):
+            wait_in(*arrays[0], t, dc)
+        here = rows(from_chip(t), block)
+        kt[:, here] = kb[here, :].T
+
+    @pl.loop(0, chips)
+    def _(i):
+        for dc in range(2):
+            wait_in(*arrays[1], turn(i), dc)
+
 
     def out_copy(a, src, dst, t, dc):
         to = device(from_chip(t), dc)
@@ -331,6 +339,18 @@
         hgs.at[rows(sec, 2 * hown)], hgr.at[rows(0, 2 * hown)], gh_recv.at[0]
     )
 
+    back = ((1, dks, gk_out), (2, dvs, gv_out))
+
+    def return_chip(t):
+        here = rows(from_chip(t), block)
+        dks[here, :] = dka[here, :].astype(BF)
+        dvs[here, :] = dva[here, :].astype(BF)
+        for a, src, dst in back:
+            start_out(a, src, dst, t)
+
+    return_chip(chips - 1)
+    return_chip(chips - 2)
+
     for i in range(secs):
         mine = slice(seq + i * hown, seq + (i + 1) * hown)
         hgs[2 * i * hown : (2 * i + 1) * hown, :] = dka[mine, :].astype(BF)
@@ -341,16 +361,9 @@
     def _(i):
         gh_copy(i).start()
 
-    back = ((1, dks, gk_out), (2, dvs, gv_out))
-
-    @pl.loop(0, chips)
-    def _(i):
-        t = chips - 1 - i
-        here = rows(from_chip(t), block)
-        dks[here, :] = dka[here, :].astype(BF)
-        dvs[here, :] = dva[here, :].astype(BF)
-        for a, src, dst in back:
-            start_out(a, src, dst, t)
+    @pl.loop(2, chips)
+    def _(i):
+        return_chip(chips - 1 - i)
 
     gh_local.wait()
 

time: 93.7 us -> 93.7 us (level)
  no operation moved by 1% of the time
where the time goes in v6:
time: 93.7 us; the launch traced here: 93.6 us
  Pallas kernels  93 us (99%)
    pallas_call x1, Pallas kernels, on_device(): pl.pallas_call(functools.partial(kernel, secs, grps), out_shape=[pltpu.VM...  91.8 us

profile of v6, /device:TPU:1, one launch (start us, length us, event | category | flops | bytes accessed | tf_op | source)
XLA Modules:
  0.0 93.6 jit_solution(9793727060426882866)
XLA Ops:
  0.6 91.8 %shard_map.93 = (bf16[128,2048]{1,0:T(8,128)(2,1)S(1)}, bf16[128,2048]{1,0:T(8,128)(2,1)S(1)}, bf16[128,2048]{1,0:T(8,128)(2,1)S(1)}, f32[128,128]{1,0:T(8,128)S(1)}) custom-call(bf16[128,2048]{1,0:T(8,128)(2,1)} %q_in.1, bf16[128,2048]{1,0:T(8,128)(2,1)} %k_in.1, bf16[128,2048]{1,0:T(8,128)(2,1)} %v_in.1, bf16[128,2048]{1,0:T(8,128)(2,1)} %g_in.1, ...), custom_call_target="tpu_custom_call" | custom-call | tf_op jit(solution)/shard_map/pallas_call | solution.py:443
  92.4 1.2 %shard_map.94 = (bf16[128,2048]{1,0:T(8,128)(2,1)}, bf16[128,2048]{1,0:T(8,128)(2,1)}, bf16[128,2048]{1,0:T(8,128)(2,1)}, f32[128,128]{1,0:T(8,128)}) custom-call(bf16[128,2048]{1,0:T(8,128)(2,1)S(1)} %get-tuple-element.12.refs_0_, bf16[128,2048]{1,0:T(8,128)(2,1)S(1)} %get-tuple-element.13.refs_1_, bf16[128,2048]{1,0:T(8,128)(2,1)S(1)} %get-tuple-element.14.refs_2_, ...), custom_call_target="tpu_custom_call" | custom-call | tf_op jit(solution)/shard_map/pallas_call | solution.py:423

commit v7 on v6

--- a/solution.py
+++ b/solution.py
@@ -195,14 +195,13 @@
                 in_copy(a, src, dst, t, 0).start()
                 in_copy(a, src, dst, t, 1).start()
 
-    start_in(0, 1)
+    start_in(0, 2)
     all_there()
 
     @pl.loop(1, secs)
     def _(i):
         h_copy(i).start()
 
-    start_in(1, 2)
     start_in(2, 4)
 
     dka[...] = jnp.zeros_like(dka)

time: 93.7 us -> 94.3 us (level)
  no operation moved by 1% of the time
where the time goes in v7:
time: 94.3 us; the launch traced here: 94.2 us
  Pallas kernels  93.6 us (99%)
    pallas_call x1, Pallas kernels, on_device(): pl.pallas_call(functools.partial(kernel, secs, grps), out_shape=[pltpu.VM...  92.4 us

profile of v7, /device:TPU:1, one launch (start us, length us, event | category | flops | bytes accessed | tf_op | source)
XLA Modules:
  0.0 94.2 jit_solution(3525689761485019134)
XLA Ops:
  0.6 92.4 %shard_map.93 = (bf16[128,2048]{1,0:T(8,128)(2,1)S(1)}, bf16[128,2048]{1,0:T(8,128)(2,1)S(1)}, bf16[128,2048]{1,0:T(8,128)(2,1)S(1)}, f32[128,128]{1,0:T(8,128)S(1)}) custom-call(bf16[128,2048]{1,0:T(8,128)(2,1)} %q_in.1, bf16[128,2048]{1,0:T(8,128)(2,1)} %k_in.1, bf16[128,2048]{1,0:T(8,128)(2,1)} %v_in.1, bf16[128,2048]{1,0:T(8,128)(2,1)} %g_in.1, ...), custom_call_target="tpu_custom_call" | custom-call | tf_op jit(solution)/shard_map/pallas_call | solution.py:442
  93.0 1.2 %shard_map.94 = (bf16[128,2048]{1,0:T(8,128)(2,1)}, bf16[128,2048]{1,0:T(8,128)(2,1)}, bf16[128,2048]{1,0:T(8,128)(2,1)}, f32[128,128]{1,0:T(8,128)}) custom-call(bf16[128,2048]{1,0:T(8,128)(2,1)S(1)} %get-tuple-element.12.refs_0_, bf16[128,2048]{1,0:T(8,128)(2,1)S(1)} %get-tuple-element.13.refs_1_, bf16[128,2048]{1,0:T(8,128)(2,1)S(1)} %get-tuple-element.14.refs_2_, ...), custom_call_target="tpu_custom_call" | custom-call | tf_op jit(solution)/shard_map/pallas_call | solution.py:422
